TPU v7x, 32 devices: a whole 2x2x4 slice. The times are simulated.
32 devices in a mesh: lat: 2 (over x), lon: 8 (over z, core), head: 2 (over y).
Axes of the slice: x: 2, y: 2, z: 4, core: 2. Of those that a mesh axis runs over, the one named last changes fastest.
Arguments:
- queries: bfloat16 [16, 384, 1024], P('lat', ('lon', 'head')), may hold values from -28 to 28
- keys_in: bfloat16 [16, 384, 1024], P('lat', ('lon', 'head')), may hold values from -28 to 28
- values: bfloat16 [16, 384, 1024], P('lat', ('lon', 'head')), may hold values from -6 to 6
- grad_out: bfloat16 [16, 384, 1024], P('lat', ('lon', 'head')), may hold values from -6 to 6
Outputs:
- attended: bfloat16 [16, 384, 1024], P('lat', ('lon', 'head'))
- grad_query: bfloat16 [16, 384, 1024], P('lat', ('lon', 'head'))
- grad_key: bfloat16 [16, 384, 1024], P('lat', ('lon', 'head'))
- grad_value: bfloat16 [16, 384, 1024], P('lat', ('lon', 'head'))
All inputs are finite; a program needn't handle non-finite values.
Results may differ from a plain program's by a relative error of at most 0.02.
Values may be sent and summed in bfloat16 or wider, within the bound.
A program may use at most 128 MiB of HBM per device.

v0:
```python
import functools

import jax
import jax.numpy as jnp
import numpy as np
from jax import lax
from jax.experimental import pallas as pl
from jax.experimental.pallas import tpu as pltpu
from jax.sharding import PartitionSpec as P

HD = 64
RAD = 6
LANES = 256
MASKED = -1e30
MESH = pl.DeviceIdType.MESH


def rounded_up(size, step):
    return -(-size // step) * step


def tables(rows, cols, slots):
    tokens, strip = rows * cols, RAD * cols
    edge = rows * RAD
    corner = rounded_up(RAD * RAD, 16)
    lead = corner - RAD * RAD
    region = 2 * corner - 16
    count = rounded_up(tokens + 2 * edge + slots * (strip + region), 128)
    where = np.zeros((count, 128), np.float32)

    def put(at, row, col, slot=None):
        where[at, 0], where[at, 1], where[at, 4] = row, col, 1
        if slot is not None:
            where[at, 2 + slot] = 1

    for i in range(tokens):
        put(i, i // cols, i % cols)
    for i in range(edge):
        put(tokens + i, i // RAD, i % RAD - RAD)
        put(tokens + edge + i, i // RAD, cols + i % RAD)
    base = tokens + 2 * edge
    for slot in range(slots):
        for i in range(strip):
            put(base + slot * strip + i, i // cols, i % cols, slot)
        start = base + slots * strip + slot * region
        for i in range(RAD * RAD):
            put(start + i, i // RAD, i % RAD - RAD, slot)
            put(start + region - RAD * RAD + i, i // RAD, cols + i % RAD, slot)
    pick_edge = np.zeros((2 * edge, tokens), np.float32)
    for i in range(edge):
        pick_edge[i, (i // RAD) * cols + cols - RAD + i % RAD] = 1
        pick_edge[edge + i, (i // RAD) * cols + i % RAD] = 1
    pick_corner = np.zeros((2 * corner, strip), np.float32)
    for i in range(RAD * RAD):
        pick_corner[i, (i // RAD) * cols + cols - RAD + i % RAD] = 1
        pick_corner[corner + lead + i, (i // RAD) * cols + i % RAD] = 1
    heads = LANES // HD
    place = np.zeros((8, heads * tokens), np.float32)
    for i in range(tokens):
        place[0, i::tokens] = i // cols
        place[1, i::tokens] = i % cols
    return where, place, pick_edge, pick_corner


def dot(a, b, a_dim=1, b_dim=0):
    return lax.dot_general(a, b, (((a_dim,), (b_dim,)), ((), ())), preferred_element_type=jnp.float32)


def kernel(
    dims, q_ref, k_ref, v_ref, g_ref, where_ref, place_ref, edge_ref, edge_t_ref, corner_ref, corner_t_ref,
    att_ref, dq_ref, dk_ref, dv_ref,
    bias, keys, got_lat, put_edge, got_edge, put_corner, got_corner, put_side, got_side, put_lat, got_back,
    own, lat_sum, lat_s, lat_r, edge_s, edge_r, corner_s, corner_r, side_s, side_r, back_s, back_r,
):
    rows, cols, slots, n_lat, n_lon, n_head, chunks = dims
    tokens, strip, edge = rows * cols, RAD * cols, rows * RAD
    corner = rounded_up(RAD * RAD, 16)
    region = 2 * corner - 16
    used = tokens + 2 * edge + slots * (strip + region)
    count = keys.shape[0]
    heads = LANES // HD
    lat, lon, head = lax.axis_index("lat"), lax.axis_index("lon"), lax.axis_index("head")
    column = lon * n_head + head
    ring = n_lon * n_head

    def beside(step):
        c = lax.rem(column + step + ring, ring)
        return (lat, c // n_head, lax.rem(c, n_head))

    right, left = beside(1), beside(-1)
    if slots == 1:
        partners = [(1 - lat, lon, head)]
        first_row = [(1 - lat) * ((rows - RAD) * cols)]
        strip_row = [rows - lat * (rows + RAD)]
        far_slot = [0]
    else:
        partners = [(lax.rem(lat + n_lat - 1, n_lat), lon, head), (lax.rem(lat + 1, n_lat), lon, head)]
        first_row = [0, (rows - RAD) * cols]
        strip_row = [-RAD, rows]
        far_slot = [1, 0]

    def strip_of(slot):
        start = first_row[slot]
        if not isinstance(start, int):
            start = pl.multiple_of(start, 16)
        return pl.ds(start, strip)

    def lanes_of(g):
        return pl.ds(pl.multiple_of(g * LANES, LANES), LANES)

    def remote(src, dst, s, r, device):
        return pltpu.make_async_remote_copy(
            src_ref=src, dst_ref=dst, send_sem=s, recv_sem=r, device_id=device, device_id_type=MESH
        )

    def lat_copies(g):
        made = []
        for slot in range(slots):
            for half, ref in enumerate((k_ref, v_ref)):
                made.append(
                    remote(
                        ref.at[strip_of(slot), lanes_of(g)],
                        got_lat.at[g, far_slot[slot], :, pl.ds(half * LANES, LANES)],
                        lat_s.at[g, 2 * slot + half], lat_r.at[g, 2 * far_slot[slot] + half], partners[slot],
                    )
                )
        return made

    def edge_copies(g):
        return [
            remote(put_edge.at[g, side], got_edge.at[g, side], edge_s.at[g, side], edge_r.at[g, side], device)
            for side, device in enumerate((right, left))
        ]

    def corner_copies(g):
        return [
            remote(
                put_corner.at[g, 2 * slot + side], got_corner.at[g, 2 * slot + side],
                corner_s.at[g, 2 * slot + side], corner_r.at[g, 2 * slot + side], device,
            )
            for slot in range(slots)
            for side, device in enumerate((right, left))
        ]

    def side_copies(g):
        return [
            remote(put_side.at[g, side], got_side.at[g, side], side_s.at[g, side], side_r.at[g, side], device)
            for side, device in enumerate((left, right))
        ]

    def back_copies(g):
        return [
            remote(
                put_lat.at[g, slot], got_back.at[g, far_slot[slot]],
                back_s.at[g, slot], back_r.at[g, far_slot[slot]], partners[slot],
            )
            for slot in range(slots)
        ]

    def send_edges(g):
        for half, ref in enumerate((k_ref, v_ref)):
            picked = dot(edge_ref[...], ref[:, lanes_of(g)]).astype(jnp.bfloat16)
            at = pl.ds(half * LANES, LANES)
            put_edge[g, 0, :, at] = picked[:edge]
            put_edge[g, 1, :, at] = picked[edge:]
        for copy in edge_copies(g):
            copy.start()

    barrier = pltpu.get_barrier_semaphore()
    for device in [left, right] + partners:
        pl.semaphore_signal(barrier, inc=1, device_id=device, device_id_type=MESH)
    pl.semaphore_wait(barrier, 2 + slots)

    def start_lat(g, carry):
        for copy in lat_copies(g):
            copy.start()
        return carry

    lax.fori_loop(0, chunks, start_lat, 0)
    send_edges(0)

    info = where_ref[...]
    key_row, key_col = info[:, 0:1], info[:, 1:2]
    for slot in range(slots):
        shift = jnp.asarray(strip_row[slot], jnp.int32).astype(jnp.float32)
        key_row = key_row + info[:, 2 + slot : 3 + slot] * shift
    lat_row = key_row + (lat * rows).astype(jnp.float32)
    valid = (info[:, 4:5] > 0.5) & (lat_row >= 0.0) & (lat_row <= float(rows * n_lat - 1))
    key_row = jnp.where(valid, key_row, 1000.0)
    near = (jnp.abs(key_row - place_ref[0:1, :]) <= RAD) & (jnp.abs(key_col - place_ref[1:2, :]) <= RAD)
    bias[...] = jnp.where(near, 0.0, MASKED)
    if count > used:
        keys[pl.ds(used, count - used), :] = jnp.zeros((count - used, 2 * LANES), jnp.bfloat16)

    lane_head = lax.broadcasted_iota(jnp.int32, (tokens, LANES), 1) // HD
    ones = [jnp.where(lane_head == h, 1.0, 0.0).astype(jnp.bfloat16) for h in range(heads)]

    def by_head(block):
        return jnp.concatenate([block * one for one in ones], axis=0)

    def from_heads(stacked):
        total = stacked[:tokens] * ones[0]
        for h in range(1, heads):
            total = total + stacked[h * tokens : (h + 1) * tokens] * ones[h]
        return total

    def spread_corners(g):
        for copy in lat_copies(g):
            copy.wait_recv()
        for slot in range(slots):
            picked = dot(corner_ref[...], got_lat[g, slot]).astype(jnp.bfloat16)
            put_corner[g, 2 * slot] = picked[:corner]
            put_corner[g, 2 * slot + 1] = picked[corner:]
        for copy in corner_copies(g):
            copy.start()

        @pl.when(g + 1 < chunks)
        def _():
            send_edges(g + 1)

    def attend(g):
        lanes = lanes_of(g)
        for copy in edge_copies(g) + corner_copies(g):
            copy.wait_recv()
        keys[pl.ds(0, tokens), pl.ds(0, LANES)] = k_ref[:, lanes]
        keys[pl.ds(0, tokens), pl.ds(LANES, LANES)] = v_ref[:, lanes]
        for side in range(2):
            keys[pl.ds(tokens + side * edge, edge), :] = got_edge[g, side]
        base = tokens + 2 * edge
        for slot in range(slots):
            keys[pl.ds(base + slot * strip, strip), :] = got_lat[g, slot]
            start = base + slots * strip + slot * region
            low, high = got_corner[g, 2 * slot], got_corner[g, 2 * slot + 1]
            keys[pl.ds(start, corner - 16), :] = low[: corner - 16]
            keys[pl.ds(start + corner - 16, 16), :] = low[corner - 16 :] + high[:16]
            keys[pl.ds(start + corner, corner - 16), :] = high[16:]
        key_block = keys[:, pl.ds(0, LANES)]
        value_block = keys[:, pl.ds(LANES, LANES)]
        query_block = by_head(q_ref[:, lanes])
        grad_block = by_head(g_ref[:, lanes])
        scale = HD ** -0.5
        scores = dot(key_block, query_block, 1, 1) * scale + bias[...]
        weights = jnp.exp(scores - jnp.max(scores, axis=0, keepdims=True))
        weights = weights * (1.0 / jnp.sum(weights, axis=0, keepdims=True))
        probabilities = weights.astype(jnp.bfloat16)
        value_term = dot(probabilities, grad_block)
        attended = dot(value_block.T, probabilities).astype(jnp.bfloat16)
        att_ref[:, lanes] = from_heads(attended.T)
        along = dot(value_block, grad_block, 1, 1)
        weights = probabilities.astype(jnp.float32)
        row_dot = jnp.sum(weights * along, axis=0, keepdims=True)
        slopes = (weights * (along - row_dot)).astype(jnp.bfloat16)
        key_term = dot(slopes, query_block) * scale
        grad_query = (dot(key_block.T, slopes) * scale).astype(jnp.bfloat16)
        dq_ref[:, lanes] = from_heads(grad_query.T)
        for half, term in enumerate((key_term, value_term)):
            at = pl.ds(half * LANES, LANES)
            own[g, :, at] = term[:tokens]
            for side in range(2):
                put_side[g, side, pl.ds(0, edge), at] = term[
                    tokens + side * edge : tokens + (side + 1) * edge
                ].astype(jnp.bfloat16)
            for slot in range(slots):
                lat_sum[g, slot, :, at] = term[base + slot * strip : base + (slot + 1) * strip]
                start = base + slots * strip + slot * region
                for side in range(2):
                    first = start + side * (corner - 16)
                    put_side[g, side, pl.ds(edge + slot * corner, corner), at] = term[
                        first : first + corner
                    ].astype(jnp.bfloat16)
        for copy in side_copies(g):
            copy.start()

    def gather_sides(g):
        for copy in side_copies(g):
            copy.wait_recv()
        low, high = got_side[g, 0], got_side[g, 1]
        own[g] += dot(edge_t_ref[...], jnp.concatenate([low[:edge], high[:edge]], axis=0))
        for slot in range(slots):
            at = edge + slot * corner
            corners = jnp.concatenate([low[at : at + corner], high[at : at + corner]], axis=0)
            total = lat_sum[g, slot] + dot(corner_t_ref[...], corners)
            put_lat[g, slot] = total.astype(jnp.bfloat16)
        for copy in back_copies(g):
            copy.start()

    def finish(g):
        for copy in back_copies(g):
            copy.wait_recv()
        for slot in range(slots):
            own[g, strip_of(slot), :] += got_back[g, slot].astype(jnp.float32)
        dk_ref[:, lanes_of(g)] = own[g, :, pl.ds(0, LANES)].astype(jnp.bfloat16)
        dv_ref[:, lanes_of(g)] = own[g, :, pl.ds(LANES, LANES)].astype(jnp.bfloat16)

    def step(t, carry):
        for delay, stage in enumerate((spread_corners, attend, gather_sides, finish)):
            pl.when((t >= delay) & (t < chunks + delay))(functools.partial(stage, t - delay))
        return carry

    lax.fori_loop(0, chunks + 3, step, 0)

    def drain(g, carry):
        for copy in lat_copies(g) + edge_copies(g) + corner_copies(g) + side_copies(g) + back_copies(g):
            copy.wait_send()
        return carry

    lax.fori_loop(0, chunks, drain, 0)


def local(sizes, queries, keys_in, values, grad_out):
    n_lat, n_lon, n_head = sizes
    rows, cols, features = queries.shape
    slots = 1 if n_lat == 2 else 2
    chunks = features // LANES
    tokens, strip, edge = rows * cols, RAD * cols, rows * RAD
    corner = rounded_up(RAD * RAD, 16)
    side = edge + slots * corner
    where, place, pick_edge, pick_corner = tables(rows, cols, slots)
    count = where.shape[0]
    wide = 2 * LANES
    bf16, f32 = jnp.bfloat16, jnp.float32
    vmem = pl.BlockSpec(memory_space=pltpu.VMEM)
    flops = 12 * count * tokens * (LANES // HD) * LANES * chunks
    sems = [(chunks, 2 * slots)] * 2 + [(chunks, 2)] * 2 + [(chunks, 2 * slots)] * 2 + [(chunks, 2)] * 2
    sems += [(chunks, slots)] * 2
    out = pl.pallas_call(
        functools.partial(kernel, (rows, cols, slots, n_lat, n_lon, n_head, chunks)),
        out_shape=[jax.ShapeDtypeStruct((tokens, features), bf16)] * 4,
        in_specs=[vmem] * 10,
        out_specs=[vmem] * 4,
        scratch_shapes=[
            pltpu.VMEM((count, place.shape[1]), f32),
            pltpu.VMEM((count, wide), bf16),
            pltpu.VMEM((chunks, slots, strip, wide), bf16),
            pltpu.VMEM((chunks, 2, edge, wide), bf16),
            pltpu.VMEM((chunks, 2, edge, wide), bf16),
            pltpu.VMEM((chunks, 2 * slots, corner, wide), bf16),
            pltpu.VMEM((chunks, 2 * slots, corner, wide), bf16),
            pltpu.VMEM((chunks, 2, side, wide), bf16),
            pltpu.VMEM((chunks, 2, side, wide), bf16),
            pltpu.VMEM((chunks, slots, strip, wide), bf16),
            pltpu.VMEM((chunks, slots, strip, wide), bf16),
            pltpu.VMEM((chunks, tokens, wide), f32),
            pltpu.VMEM((chunks, slots, strip, wide), f32),
        ]
        + [pltpu.SemaphoreType.DMA(shape) for shape in sems],
        compiler_params=pltpu.CompilerParams(
            collective_id=0, has_side_effects=True, vmem_limit_bytes=50 * 1024 * 1024
        ),
        cost_estimate=pl.CostEstimate(flops=flops, bytes_accessed=8 * tokens * features * 2, transcendentals=0),
    )(
        *(x.reshape(tokens, features) for x in (queries, keys_in, values, grad_out)),
        jnp.asarray(where), jnp.asarray(place),
        jnp.asarray(pick_edge, bf16), jnp.asarray(np.ascontiguousarray(pick_edge.T), bf16),
        jnp.asarray(pick_corner, bf16), jnp.asarray(np.ascontiguousarray(pick_corner.T), bf16),
    )
    return tuple(x.reshape(rows, cols, features) for x in out)


def solution(mesh):
    spec = P("lat", ("lon", "head"), None)
    sizes = tuple(mesh.shape[axis] for axis in ("lat", "lon", "head"))
    return jax.shard_map(
        functools.partial(local, sizes), mesh=mesh, in_specs=(spec,) * 4, out_specs=(spec,) * 4, check_vma=False
    )
```

profile of v0, /device:TPU:0, one launch (start us, length us, event | category | flops | bytes accessed | tf_op | source)
XLA Modules:
  0.0 60.1 jit_solution(18360671674980835807)
XLA Ops:
  0.6 0.0 copy-start
  0.6 1.0 %copy-done = bf16[8,24,1024]{2,1,0:T(8,128)(2,1)S(1)} copy-done((bf16[8,24,1024]{2,1,0:T(8,128)(2,1)S(1)}, bf16[8,24,1024]{2,1,0:T(8,128)(2,1)}, u32[]{:S(2)}) %copy-start) | copy-done | bytes 393240
  1.6 0.0 copy-start.1
  1.6 1.0 %copy-done.1 = bf16[8,24,1024]{2,1,0:T(8,128)(2,1)S(1)} copy-done((bf16[8,24,1024]{2,1,0:T(8,128)(2,1)S(1)}, bf16[8,24,1024]{2,1,0:T(8,128)(2,1)}, u32[]{:S(2)}) %copy-start.1) | copy-done | bytes 393240
  2.6 0.0 copy-start.2
  2.6 1.0 %copy-done.2 = bf16[8,24,1024]{2,1,0:T(8,128)(2,1)S(1)} copy-done((bf16[8,24,1024]{2,1,0:T(8,128)(2,1)S(1)}, bf16[8,24,1024]{2,1,0:T(8,128)(2,1)}, u32[]{:S(2)}) %copy-start.2) | copy-done | bytes 393240
  3.6 0.0 copy-start.3
  3.6 1.0 %copy-done.3 = bf16[8,24,1024]{2,1,0:T(8,128)(2,1)S(1)} copy-done((bf16[8,24,1024]{2,1,0:T(8,128)(2,1)S(1)}, bf16[8,24,1024]{2,1,0:T(8,128)(2,1)}, u32[]{:S(2)}) %copy-start.3) | copy-done | bytes 393240
  4.6 0.0 copy-start.4
  4.6 0.9 %copy-done.4 = f32[512,128]{1,0:T(8,128)S(1)} copy-done((f32[512,128]{1,0:T(8,128)S(1)}, f32[512,128]{1,0:T(8,128)}, u32[]{:S(2)}) %copy-start.4) | copy-done | bytes 262168
  5.6 0.0 copy-start.5
  5.6 0.8 %copy-done.5 = bf16[96,144]{1,0:T(8,128)(2,1)S(1)} copy-done((bf16[96,144]{1,0:T(8,128)(2,1)S(1)}, bf16[96,144]{1,0:T(8,128)(2,1)}, u32[]{:S(2)}) %copy-start.5) | copy-done | bytes 27672
  6.4 0.0 copy-start.6
  6.4 0.8 %copy-done.6 = bf16[192,96]{1,0:T(8,128)(2,1)S(1)} copy-done((bf16[192,96]{1,0:T(8,128)(2,1)S(1)}, bf16[192,96]{1,0:T(8,128)(2,1)}, u32[]{:S(2)}) %copy-start.6) | copy-done | bytes 36888
  7.2 0.0 copy-start.7
  7.2 0.8 %copy-done.7 = bf16[96,192]{1,0:T(8,128)(2,1)S(1)} copy-done((bf16[96,192]{1,0:T(8,128)(2,1)S(1)}, bf16[96,192]{1,0:T(8,128)(2,1)}, u32[]{:S(2)}) %copy-start.7) | copy-done | bytes 36888
  8.0 0.0 copy-start.8
  8.0 0.8 %copy-done.8 = bf16[144,96]{1,0:T(8,128)(2,1)S(1)} copy-done((bf16[144,96]{1,0:T(8,128)(2,1)S(1)}, bf16[144,96]{1,0:T(8,128)(2,1)}, u32[]{:S(2)}) %copy-start.8) | copy-done | bytes 27672
  8.7 0.0 copy-start.9
  8.7 0.7 %copy-done.9 = f32[8,768]{1,0:T(8,128)S(1)} copy-done((f32[8,768]{1,0:T(8,128)S(1)}, f32[8,768]{1,0:T(8,128)}, u32[]{:S(2)}) %copy-start.9) | copy-done | bytes 24600
  9.5 47.6 %shard_map.129 = (bf16[192,1024]{1,0:T(8,128)(2,1)S(1)}, bf16[192,1024]{1,0:T(8,128)(2,1)S(1)}, bf16[192,1024]{1,0:T(8,128)(2,1)S(1)}, bf16[192,1024]{1,0:T(8,128)(2,1)S(1)}) custom-call(bf16[192,1024]{1,0:T(8,128)(2,1)S(1)} %bitcast.12, bf16[192,1024]{1,0:T(8,128)(2,1)S(1)} %bitcast.13, bf16[192,1024]{1,0:T(8,128)(2,1)S(1)} %bitcast.14, ...), custom_call_target="tpu_custom_call" | custom-call | flops 4831838208 | bytes 3145728 | tf_op jit(solution)/shard_map/pallas_call | solution.py:326
  57.1 0.7 %copy.18 = bf16[8,24,1024]{2,1,0:T(8,128)(2,1)} copy(bf16[8,24,1024]{2,1,0:T(8,128)(2,1)S(1)} %bitcast.11) | data formatting | bytes 786432
  57.8 0.7 %copy.19 = bf16[8,24,1024]{2,1,0:T(8,128)(2,1)} copy(bf16[8,24,1024]{2,1,0:T(8,128)(2,1)S(1)} %bitcast.10) | data formatting | bytes 786432
  58.6 0.7 %copy.20 = bf16[8,24,1024]{2,1,0:T(8,128)(2,1)} copy(bf16[8,24,1024]{2,1,0:T(8,128)(2,1)S(1)} %bitcast.9) | data formatting | bytes 786432
  59.3 0.7 %copy.21 = bf16[8,24,1024]{2,1,0:T(8,128)(2,1)} copy(bf16[8,24,1024]{2,1,0:T(8,128)(2,1)S(1)} %bitcast.8) | data formatting | bytes 786432
Async XLA Ops:
  0.6 1.0 %copy-start = (bf16[8,24,1024]{2,1,0:T(8,128)(2,1)S(1)}, bf16[8,24,1024]{2,1,0:T(8,128)(2,1)}, u32[]{:S(2)}) copy-start(bf16[8,24,1024]{2,1,0:T(8,128)(2,1)} %param.10) | copy-start | bytes 1179652
  1.6 1.0 %copy-start.1 = (bf16[8,24,1024]{2,1,0:T(8,128)(2,1)S(1)}, bf16[8,24,1024]{2,1,0:T(8,128)(2,1)}, u32[]{:S(2)}) copy-start(bf16[8,24,1024]{2,1,0:T(8,128)(2,1)} %param.11) | copy-start | bytes 1179652
  2.6 1.0 %copy-start.2 = (bf16[8,24,1024]{2,1,0:T(8,128)(2,1)S(1)}, bf16[8,24,1024]{2,1,0:T(8,128)(2,1)}, u32[]{:S(2)}) copy-start(bf16[8,24,1024]{2,1,0:T(8,128)(2,1)} %param.12) | copy-start | bytes 1179652
  3.6 1.0 %copy-start.3 = (bf16[8,24,1024]{2,1,0:T(8,128)(2,1)S(1)}, bf16[8,24,1024]{2,1,0:T(8,128)(2,1)}, u32[]{:S(2)}) copy-start(bf16[8,24,1024]{2,1,0:T(8,128)(2,1)} %param.13) | copy-start | bytes 1179652
  4.6 0.9 %copy-start.4 = (f32[512,128]{1,0:T(8,128)S(1)}, f32[512,128]{1,0:T(8,128)}, u32[]{:S(2)}) copy-start(f32[512,128]{1,0:T(8,128)} %constant.12.clone.where_ref) | copy-start | bytes 786436
  5.6 0.8 %copy-start.5 = (bf16[96,144]{1,0:T(8,128)(2,1)S(1)}, bf16[96,144]{1,0:T(8,128)(2,1)}, u32[]{:S(2)}) copy-start(bf16[96,144]{1,0:T(8,128)(2,1)} %constant.16.clone.corner_ref) | copy-start | bytes 82948
  6.4 0.8 %copy-start.6 = (bf16[192,96]{1,0:T(8,128)(2,1)S(1)}, bf16[192,96]{1,0:T(8,128)(2,1)}, u32[]{:S(2)}) copy-start(bf16[192,96]{1,0:T(8,128)(2,1)} %constant.15.clone.edge_t_ref) | copy-start | bytes 110596
  7.2 0.8 %copy-start.7 = (bf16[96,192]{1,0:T(8,128)(2,1)S(1)}, bf16[96,192]{1,0:T(8,128)(2,1)}, u32[]{:S(2)}) copy-start(bf16[96,192]{1,0:T(8,128)(2,1)} %constant.14.clone.edge_ref) | copy-start | bytes 110596
  8.0 0.8 %copy-start.8 = (bf16[144,96]{1,0:T(8,128)(2,1)S(1)}, bf16[144,96]{1,0:T(8,128)(2,1)}, u32[]{:S(2)}) copy-start(bf16[144,96]{1,0:T(8,128)(2,1)} %constant.17.clone.corner_t_ref) | copy-start | bytes 82948
  8.7 0.7 %copy-start.9 = (f32[8,768]{1,0:T(8,128)S(1)}, f32[8,768]{1,0:T(8,128)}, u32[]{:S(2)}) copy-start(f32[8,768]{1,0:T(8,128)} %constant.13.clone.place_ref) | copy-start | bytes 73732
where the time goes:
time: 60.8 us; the launch traced here: 60.1 us
  Pallas kernels  47.6 us (78%)
  local copies, waits for them, and re-layouts  11.8 us (19%)
  between operations  0.66 us (1%)
    pallas_call x1, Pallas kernels, local(): pl.pallas_call(functools.partial(kernel, (rows, cols, slots, n_lat, n_lon...  47.6 us
    unnamed x24, local copies, waits for them, and re-layouts  11.8 us

commit v1 on v0

--- a/solution.py
+++ b/solution.py
@@ -2,7 +2,6 @@
 
 import jax
 import jax.numpy as jnp
-import numpy as np
 from jax import lax
 from jax.experimental import pallas as pl
 from jax.experimental.pallas import tpu as pltpu
@@ -19,47 +18,62 @@
     return -(-size // step) * step
 
 
-def tables(rows, cols, slots):
-    tokens, strip = rows * cols, RAD * cols
-    edge = rows * RAD
+def floor_div(i, n):
+    return jnp.floor((i + 0.5) * (1.0 / n))
+
+
+def counted(shape, dim):
+    return lax.broadcasted_iota(jnp.int32, shape, dim).astype(jnp.float32)
+
+
+def edge_token(i, count, cols):
+    first = jnp.where(i < count, cols - RAD, 0.0)
+    i = jnp.where(i < count, i, i - count)
+    row = floor_div(i, RAD)
+    return row * cols + (i - row * RAD) + first
+
+
+def corner_token(i, corner, cols):
+    size = RAD * RAD
+    lead = corner - size
+    token = edge_token(jnp.where(i < corner, i, i - corner - lead + size), size, cols)
+    real = (i < size) | (i >= corner + lead)
+    return jnp.where(real, token, -1.0)
+
+
+def key_places(count, rows, cols, strip_row):
+    slots = len(strip_row)
+    tokens, strip, edge = rows * cols, RAD * cols, rows * RAD
     corner = rounded_up(RAD * RAD, 16)
-    lead = corner - RAD * RAD
     region = 2 * corner - 16
-    count = rounded_up(tokens + 2 * edge + slots * (strip + region), 128)
-    where = np.zeros((count, 128), np.float32)
-
-    def put(at, row, col, slot=None):
-        where[at, 0], where[at, 1], where[at, 4] = row, col, 1
-        if slot is not None:
-            where[at, 2 + slot] = 1
-
-    for i in range(tokens):
-        put(i, i // cols, i % cols)
-    for i in range(edge):
-        put(tokens + i, i // RAD, i % RAD - RAD)
-        put(tokens + edge + i, i // RAD, cols + i % RAD)
+    i = counted((count, 1), 0)
+    row = floor_div(i, cols)
+    col = i - row * cols
+    real = jnp.where(i < tokens + 2 * edge + slots * (strip + region), 1.0, 0.0)
+    for side in range(2):
+        at = i - (tokens + side * edge)
+        here = (at >= 0) & (at < edge)
+        r = floor_div(at, RAD)
+        row = jnp.where(here, r, row)
+        col = jnp.where(here, at - r * RAD + (cols if side else -RAD), col)
     base = tokens + 2 * edge
     for slot in range(slots):
-        for i in range(strip):
-            put(base + slot * strip + i, i // cols, i % cols, slot)
-        start = base + slots * strip + slot * region
-        for i in range(RAD * RAD):
-            put(start + i, i // RAD, i % RAD - RAD, slot)
-            put(start + region - RAD * RAD + i, i // RAD, cols + i % RAD, slot)
-    pick_edge = np.zeros((2 * edge, tokens), np.float32)
-    for i in range(edge):
-        pick_edge[i, (i // RAD) * cols + cols - RAD + i % RAD] = 1
-        pick_edge[edge + i, (i // RAD) * cols + i % RAD] = 1
-    pick_corner = np.zeros((2 * corner, strip), np.float32)
-    for i in range(RAD * RAD):
-        pick_corner[i, (i // RAD) * cols + cols - RAD + i % RAD] = 1
-        pick_corner[corner + lead + i, (i // RAD) * cols + i % RAD] = 1
-    heads = LANES // HD
-    place = np.zeros((8, heads * tokens), np.float32)
-    for i in range(tokens):
-        place[0, i::tokens] = i // cols
-        place[1, i::tokens] = i % cols
-    return where, place, pick_edge, pick_corner
+        top = jnp.asarray(strip_row[slot], jnp.int32).astype(jnp.float32)
+        at = i - (base + slot * strip)
+        here = (at >= 0) & (at < strip)
+        r = floor_div(at, cols)
+        row = jnp.where(here, r + top, row)
+        col = jnp.where(here, at - r * cols, col)
+        for side in range(2):
+            start = base + slots * strip + slot * region
+            at = i - (start + side * (region - RAD * RAD))
+            here = (at >= 0) & (at < RAD * RAD)
+            r = floor_div(at, RAD)
+            row = jnp.where(here, r + top, row)
+            col = jnp.where(here, at - r * RAD + (cols if side else -RAD), col)
+        at = i - (base + slots * strip + slot * region)
+        real = jnp.where((at >= RAD * RAD) & (at < region - RAD * RAD), 0.0, real)
+    return row, col, real > 0.5
 
 
 def dot(a, b, a_dim=1, b_dim=0):
@@ -67,10 +81,9 @@
 
 
 def kernel(
-    dims, q_ref, k_ref, v_ref, g_ref, where_ref, place_ref, edge_ref, edge_t_ref, corner_ref, corner_t_ref,
-    att_ref, dq_ref, dk_ref, dv_ref,
-    bias, keys, got_lat, put_edge, got_edge, put_corner, got_corner, put_side, got_side, put_lat, got_back,
-    own, lat_sum, lat_s, lat_r, edge_s, edge_r, corner_s, corner_r, side_s, side_r, back_s, back_r,
+    dims, q_hbm, k_hbm, v_hbm, g_hbm, att_hbm, dq_hbm, dk_hbm, dv_hbm,
+    att_ref, dq_ref, dk_ref, dv_ref, q_ref, k_ref, v_ref, g_ref, edge_ref, edge_t_ref, corner_ref, corner_t_ref, bias, keys, got_lat, put_edge, got_edge, put_corner, got_corner, put_side, got_side, put_lat, got_back,
+    own, lat_sum, load_sem, save_sem, lat_s, lat_r, edge_s, edge_r, corner_s, corner_r, side_s, side_r, back_s, back_r,
 ):
     rows, cols, slots, n_lat, n_lon, n_head, chunks = dims
     tokens, strip, edge = rows * cols, RAD * cols, rows * RAD
@@ -116,7 +129,7 @@
     def lat_copies(g):
         made = []
         for slot in range(slots):
-            for half, ref in enumerate((k_ref, v_ref)):
+            for half, ref in enumerate((k_hbm, v_hbm)):
                 made.append(
                     remote(
                         ref.at[strip_of(slot), lanes_of(g)],
@@ -157,6 +170,13 @@
             for slot in range(slots)
         ]
 
+    def saves(g, first):
+        pairs = ((att_ref, att_hbm), (dq_ref, dq_hbm), (dk_ref, dk_hbm), (dv_ref, dv_hbm))
+        return [
+            pltpu.make_async_copy(src.at[:, lanes_of(g)], dst.at[:, lanes_of(g)], save_sem.at[g, first + n])
+            for n, (src, dst) in enumerate(pairs[first : first + 2])
+        ]
+
     def send_edges(g):
         for half, ref in enumerate((k_ref, v_ref)):
             picked = dot(edge_ref[...], ref[:, lanes_of(g)]).astype(jnp.bfloat16)
@@ -166,6 +186,12 @@
         for copy in edge_copies(g):
             copy.start()
 
+    loads = [
+        pltpu.make_async_copy(src, dst, load_sem.at[n])
+        for n, (src, dst) in enumerate(((k_hbm, k_ref), (v_hbm, v_ref), (q_hbm, q_ref), (g_hbm, g_ref)))
+    ]
+    for load in loads:
+        load.start()
     barrier = pltpu.get_barrier_semaphore()
     for device in [left, right] + partners:
         pl.semaphore_signal(barrier, inc=1, device_id=device, device_id_type=MESH)
@@ -177,21 +203,34 @@
         return carry
 
     lax.fori_loop(0, chunks, start_lat, 0)
+
+    def one_hot(token, place):
+        return jnp.where(token == place, 1.0, 0.0).astype(jnp.bfloat16)
+
+    n = 2 * edge
+    edge_ref[...] = one_hot(edge_token(counted((n, 1), 0), edge, cols), counted((n, tokens), 1))
+    loads[0].wait()
+    loads[1].wait()
     send_edges(0)
-
-    info = where_ref[...]
-    key_row, key_col = info[:, 0:1], info[:, 1:2]
-    for slot in range(slots):
-        shift = jnp.asarray(strip_row[slot], jnp.int32).astype(jnp.float32)
-        key_row = key_row + info[:, 2 + slot : 3 + slot] * shift
+    edge_t_ref[...] = one_hot(edge_token(counted((1, n), 1), edge, cols), counted((tokens, n), 0))
+    n = 2 * corner
+    corner_ref[...] = one_hot(corner_token(counted((n, 1), 0), corner, cols), counted((n, strip), 1))
+    corner_t_ref[...] = one_hot(corner_token(counted((1, n), 1), corner, cols), counted((strip, n), 0))
+    key_row, key_col, real = key_places(count, rows, cols, strip_row)
     lat_row = key_row + (lat * rows).astype(jnp.float32)
-    valid = (info[:, 4:5] > 0.5) & (lat_row >= 0.0) & (lat_row <= float(rows * n_lat - 1))
+    valid = real & (lat_row >= 0.0) & (lat_row <= float(rows * n_lat - 1))
     key_row = jnp.where(valid, key_row, 1000.0)
-    near = (jnp.abs(key_row - place_ref[0:1, :]) <= RAD) & (jnp.abs(key_col - place_ref[1:2, :]) <= RAD)
+    place = counted((1, heads * tokens), 1)
+    place = place - floor_div(place, tokens) * tokens
+    place_row = floor_div(place, cols)
+    place_col = place - place_row * cols
+    near = (jnp.abs(key_row - place_row) <= RAD) & (jnp.abs(key_col - place_col) <= RAD)
     bias[...] = jnp.where(near, 0.0, MASKED)
     if count > used:
         keys[pl.ds(used, count - used), :] = jnp.zeros((count - used, 2 * LANES), jnp.bfloat16)
 
+    loads[2].wait()
+    loads[3].wait()
     lane_head = lax.broadcasted_iota(jnp.int32, (tokens, LANES), 1) // HD
     ones = [jnp.where(lane_head == h, 1.0, 0.0).astype(jnp.bfloat16) for h in range(heads)]
 
@@ -244,15 +283,11 @@
         weights = weights * (1.0 / jnp.sum(weights, axis=0, keepdims=True))
         probabilities = weights.astype(jnp.bfloat16)
         value_term = dot(probabilities, grad_block)
-        attended = dot(value_block.T, probabilities).astype(jnp.bfloat16)
-        att_ref[:, lanes] = from_heads(attended.T)
         along = dot(value_block, grad_block, 1, 1)
         weights = probabilities.astype(jnp.float32)
         row_dot = jnp.sum(weights * along, axis=0, keepdims=True)
         slopes = (weights * (along - row_dot)).astype(jnp.bfloat16)
         key_term = dot(slopes, query_block) * scale
-        grad_query = (dot(key_block.T, slopes) * scale).astype(jnp.bfloat16)
-        dq_ref[:, lanes] = from_heads(grad_query.T)
         for half, term in enumerate((key_term, value_term)):
             at = pl.ds(half * LANES, LANES)
             own[g, :, at] = term[:tokens]
@@ -270,6 +305,12 @@
                     ].astype(jnp.bfloat16)
         for copy in side_copies(g):
             copy.start()
+        attended = dot(value_block.T, probabilities).astype(jnp.bfloat16)
+        att_ref[:, lanes] = from_heads(attended.T)
+        grad_query = (dot(key_block.T, slopes) * scale).astype(jnp.bfloat16)
+        dq_ref[:, lanes] = from_heads(grad_query.T)
+        for copy in saves(g, 0):
+            copy.start()
 
     def gather_sides(g):
         for copy in side_copies(g):
@@ -291,6 +332,8 @@
             own[g, strip_of(slot), :] += got_back[g, slot].astype(jnp.float32)
         dk_ref[:, lanes_of(g)] = own[g, :, pl.ds(0, LANES)].astype(jnp.bfloat16)
         dv_ref[:, lanes_of(g)] = own[g, :, pl.ds(LANES, LANES)].astype(jnp.bfloat16)
+        for copy in saves(g, 2):
+            copy.start()
 
     def step(t, carry):
         for delay, stage in enumerate((spread_corners, attend, gather_sides, finish)):
@@ -302,9 +345,20 @@
     def drain(g, carry):
         for copy in lat_copies(g) + edge_copies(g) + corner_copies(g) + side_copies(g) + back_copies(g):
             copy.wait_send()
+        for copy in saves(g, 0) + saves(g, 2):
+            copy.wait()
         return carry
 
     lax.fori_loop(0, chunks, drain, 0)
+
+
+def store(a_in, b_in, c_in, d_in, a_out, b_out, c_out, d_out, sem):
+    pairs = ((a_in, a_out), (b_in, b_out), (c_in, c_out), (d_in, d_out))
+    copies = [pltpu.make_async_copy(src, dst, sem.at[n]) for n, (src, dst) in enumerate(pairs)]
+    for copy in copies:
+        copy.start()
+    for copy in copies:
+        copy.wait()
 
 
 def local(sizes, queries, keys_in, values, grad_out):
@@ -315,21 +369,25 @@
     tokens, strip, edge = rows * cols, RAD * cols, rows * RAD
     corner = rounded_up(RAD * RAD, 16)
     side = edge + slots * corner
-    where, place, pick_edge, pick_corner = tables(rows, cols, slots)
-    count = where.shape[0]
+    count = rounded_up(tokens + 2 * edge + slots * (strip + 2 * corner - 16), 128)
     wide = 2 * LANES
     bf16, f32 = jnp.bfloat16, jnp.float32
-    vmem = pl.BlockSpec(memory_space=pltpu.VMEM)
+    hbm = pl.BlockSpec(memory_space=pltpu.HBM)
     flops = 12 * count * tokens * (LANES // HD) * LANES * chunks
-    sems = [(chunks, 2 * slots)] * 2 + [(chunks, 2)] * 2 + [(chunks, 2 * slots)] * 2 + [(chunks, 2)] * 2
+    sems = [(4,), (chunks, 4)] + [(chunks, 2 * slots)] * 2 + [(chunks, 2)] * 2 + [(chunks, 2 * slots)] * 2 + [(chunks, 2)] * 2
     sems += [(chunks, slots)] * 2
     out = pl.pallas_call(
         functools.partial(kernel, (rows, cols, slots, n_lat, n_lon, n_head, chunks)),
         out_shape=[jax.ShapeDtypeStruct((tokens, features), bf16)] * 4,
-        in_specs=[vmem] * 10,
-        out_specs=[vmem] * 4,
+        in_specs=[hbm] * 4,
+        out_specs=[hbm] * 4,
         scratch_shapes=[
-            pltpu.VMEM((count, place.shape[1]), f32),
+            *[pltpu.VMEM((tokens, features), bf16)] * 8,
+            pltpu.VMEM((2 * edge, tokens), bf16),
+            pltpu.VMEM((tokens, 2 * edge), bf16),
+            pltpu.VMEM((2 * corner, strip), bf16),
+            pltpu.VMEM((strip, 2 * corner), bf16),
+            pltpu.VMEM((count, LANES // HD * tokens), f32),
             pltpu.VMEM((count, wide), bf16),
             pltpu.VMEM((chunks, slots, strip, wide), bf16),
             pltpu.VMEM((chunks, 2, edge, wide), bf16),
@@ -345,15 +403,20 @@
         ]
         + [pltpu.SemaphoreType.DMA(shape) for shape in sems],
         compiler_params=pltpu.CompilerParams(
-            collective_id=0, has_side_effects=True, vmem_limit_bytes=50 * 1024 * 1024
+            collective_id=0, has_side_effects=True, vmem_limit_bytes=64 * 1024 * 1024
         ),
         cost_estimate=pl.CostEstimate(flops=flops, bytes_accessed=8 * tokens * features * 2, transcendentals=0),
     )(
         *(x.reshape(tokens, features) for x in (queries, keys_in, values, grad_out)),
-        jnp.asarray(where), jnp.asarray(place),
-        jnp.asarray(pick_edge, bf16), jnp.asarray(np.ascontiguousarray(pick_edge.T), bf16),
-        jnp.asarray(pick_corner, bf16), jnp.asarray(np.ascontiguousarray(pick_corner.T), bf16),
     )
+    out = pl.pallas_call(
+        store,
+        out_shape=[jax.ShapeDtypeStruct((tokens, features), bf16)] * 4,
+        in_specs=[hbm] * 4,
+        out_specs=[hbm] * 4,
+        scratch_shapes=[pltpu.SemaphoreType.DMA((4,))],
+        compiler_params=pltpu.CompilerParams(vmem_limit_bytes=64 * 1024 * 1024),
+    )(*out)
     return tuple(x.reshape(rows, cols, features) for x in out)
 
 

time: 60.8 us -> 98.4 us (1.62)
  Pallas kernels: 47.6 us -> 97.7 us
  local copies, waits for them, and re-layouts: 11.8 us -> 0 us
    pallas_call x0 -> x1, Pallas kernels: none -> 48.8 us  [local(): pl.pallas_call(store, out_shape=[jax.ShapeDtypeStruct((tokens, features),...]
    unnamed x24 -> x0, local copies, waits for them, and re-layouts: 11.8 us -> none
    pallas_call x1, Pallas kernels: 47.6 us -> 48.9 us  [local(): pl.pallas_call(functools.partial(kernel, (rows, cols, slots, n_lat, n_lon...]
where the time goes in v1:
time: 98.4 us; the launch traced here: 98.3 us
  Pallas kernels  97.7 us (99%)
    pallas_call x1, Pallas kernels, local(): pl.pallas_call(functools.partial(kernel, (rows, cols, slots, n_lat, n_lon...  48.9 us
    pallas_call x1, Pallas kernels, local(): pl.pallas_call(store, out_shape=[jax.ShapeDtypeStruct((tokens, features),...  48.8 us

profile of v1, /device:TPU:0, one launch (start us, length us, event | category | flops | bytes accessed | tf_op | source)
XLA Modules:
  0.0 98.3 jit_solution(11852142802301317421)
XLA Ops:
  0.6 48.9 %shard_map.75 = (bf16[192,1024]{1,0:T(8,128)(2,1)}, bf16[192,1024]{1,0:T(8,128)(2,1)}, bf16[192,1024]{1,0:T(8,128)(2,1)}, bf16[192,1024]{1,0:T(8,128)(2,1)}) custom-call(bf16[192,1024]{1,0:T(8,128)(2,1)} %bitcast.8, bf16[192,1024]{1,0:T(8,128)(2,1)} %bitcast.9, bf16[192,1024]{1,0:T(8,128)(2,1)} %bitcast.10, bf16[192,1024]{1,0:T(8,128)(2,1)} %bitcast.11), custom_call_target="tpu_custom_call" | custom-call | flops 4831838208 | bytes 3145728 | tf_op jit(solution)/shard_map/pallas_call | solution.py:379
  49.5 48.8 %shard_map.76 = (bf16[192,1024]{1,0:T(8,128)(2,1)}, bf16[192,1024]{1,0:T(8,128)(2,1)}, bf16[192,1024]{1,0:T(8,128)(2,1)}, bf16[192,1024]{1,0:T(8,128)(2,1)}) custom-call(bf16[192,1024]{1,0:T(8,128)(2,1)} %get-tuple-element.12.a_in, bf16[192,1024]{1,0:T(8,128)(2,1)} %get-tuple-element.13.b_in, bf16[192,1024]{1,0:T(8,128)(2,1)} %get-tuple-element.14.c_in, ...), custom_call_target="tpu_custom_call" | custom-call | tf_op jit(solution)/shard_map/pallas_call | solution.py:412

commit v2 on v1

--- a/solution.py
+++ b/solution.py
@@ -9,7 +9,8 @@
 
 HD = 64
 RAD = 6
-LANES = 256
+LANES = 128
+AHEAD = 3
 MASKED = -1e30
 MESH = pl.DeviceIdType.MESH
 
@@ -202,7 +203,8 @@
             copy.start()
         return carry
 
-    lax.fori_loop(0, chunks, start_lat, 0)
+    ahead = min(AHEAD, chunks)
+    lax.fori_loop(0, ahead, start_lat, 0)
 
     def one_hot(token, place):
         return jnp.where(token == place, 1.0, 0.0).astype(jnp.bfloat16)
@@ -211,7 +213,8 @@
     edge_ref[...] = one_hot(edge_token(counted((n, 1), 0), edge, cols), counted((n, tokens), 1))
     loads[0].wait()
     loads[1].wait()
-    send_edges(0)
+    for g in range(ahead):
+        send_edges(g)
     edge_t_ref[...] = one_hot(edge_token(counted((1, n), 1), edge, cols), counted((tokens, n), 0))
     n = 2 * corner
     corner_ref[...] = one_hot(corner_token(counted((n, 1), 0), corner, cols), counted((n, strip), 1))
@@ -253,9 +256,10 @@
         for copy in corner_copies(g):
             copy.start()
 
-        @pl.when(g + 1 < chunks)
+        @pl.when(g + ahead < chunks)
         def _():
-            send_edges(g + 1)
+            start_lat(g + ahead, 0)
+            send_edges(g + ahead)
 
     def attend(g):
         lanes = lanes_of(g)
@@ -336,11 +340,11 @@
             copy.start()
 
     def step(t, carry):
-        for delay, stage in enumerate((spread_corners, attend, gather_sides, finish)):
+        for delay, stage in ((0, spread_corners), (1, attend), (3, gather_sides), (5, finish)):
             pl.when((t >= delay) & (t < chunks + delay))(functools.partial(stage, t - delay))
         return carry
 
-    lax.fori_loop(0, chunks + 3, step, 0)
+    lax.fori_loop(0, chunks + 5, step, 0)
 
     def drain(g, carry):
         for copy in lat_copies(g) + edge_copies(g) + corner_copies(g) + side_copies(g) + back_copies(g):
@@ -352,13 +356,17 @@
     lax.fori_loop(0, chunks, drain, 0)
 
 
-def store(a_in, b_in, c_in, d_in, a_out, b_out, c_out, d_out, sem):
+def store(a_in, b_in, c_in, d_in, a_out, b_out, c_out, d_out, held, in_sem, out_sem):
     pairs = ((a_in, a_out), (b_in, b_out), (c_in, c_out), (d_in, d_out))
-    copies = [pltpu.make_async_copy(src, dst, sem.at[n]) for n, (src, dst) in enumerate(pairs)]
-    for copy in copies:
-        copy.start()
-    for copy in copies:
-        copy.wait()
+    loads = [pltpu.make_async_copy(src, held.at[n], in_sem.at[n]) for n, (src, _) in enumerate(pairs)]
+    saves = [pltpu.make_async_copy(held.at[n], dst, out_sem.at[n]) for n, (_, dst) in enumerate(pairs)]
+    for load in loads:
+        load.start()
+    for load, save in zip(loads, saves):
+        load.wait()
+        save.start()
+    for save in saves:
+        save.wait()
 
 
 def local(sizes, queries, keys_in, values, grad_out):
@@ -414,7 +422,7 @@
         out_shape=[jax.ShapeDtypeStruct((tokens, features), bf16)] * 4,
         in_specs=[hbm] * 4,
         out_specs=[hbm] * 4,
-        scratch_shapes=[pltpu.SemaphoreType.DMA((4,))],
+        scratch_shapes=[pltpu.VMEM((4, tokens, features), bf16)] + [pltpu.SemaphoreType.DMA((4,))] * 2,
         compiler_params=pltpu.CompilerParams(vmem_limit_bytes=64 * 1024 * 1024),
     )(*out)
     return tuple(x.reshape(rows, cols, features) for x in out)

time: 98.4 us -> 51.4 us (0.52)
  Pallas kernels: 97.7 us -> 50.6 us
    pallas_call x1, Pallas kernels: 48.8 us -> 2.2 us  [local(): pl.pallas_call(store, out_shape=[jax.ShapeDtypeStruct((tokens, features),...]
where the time goes in v2:
time: 51.4 us; the launch traced here: 51.3 us
  Pallas kernels  50.6 us (98%)
  between operations  0.64 us (1%)
    pallas_call x1, Pallas kernels, local(): pl.pallas_call(functools.partial(kernel, (rows, cols, slots, n_lat, n_lon...  48.4 us
    pallas_call x1, Pallas kernels, local(): pl.pallas_call(store, out_shape=[jax.ShapeDtypeStruct((tokens, features),...  2.2 us

profile of v2, /device:TPU:0, one launch (start us, length us, event | category | flops | bytes accessed | tf_op | source)
XLA Modules:
  0.0 51.3 jit_solution(9924998388880744990)
XLA Ops:
  0.6 48.4 %shard_map.75 = (bf16[192,1024]{1,0:T(8,128)(2,1)}, bf16[192,1024]{1,0:T(8,128)(2,1)}, bf16[192,1024]{1,0:T(8,128)(2,1)}, bf16[192,1024]{1,0:T(8,128)(2,1)}) custom-call(bf16[192,1024]{1,0:T(8,128)(2,1)} %bitcast.8, bf16[192,1024]{1,0:T(8,128)(2,1)} %bitcast.9, bf16[192,1024]{1,0:T(8,128)(2,1)} %bitcast.10, bf16[192,1024]{1,0:T(8,128)(2,1)} %bitcast.11), custom_call_target="tpu_custom_call" | custom-call | flops 2415919104 | bytes 3145728 | tf_op jit(solution)/shard_map/pallas_call | solution.py:387
  49.1 2.2 %shard_map.76 = (bf16[192,1024]{1,0:T(8,128)(2,1)}, bf16[192,1024]{1,0:T(8,128)(2,1)}, bf16[192,1024]{1,0:T(8,128)(2,1)}, bf16[192,1024]{1,0:T(8,128)(2,1)}) custom-call(bf16[192,1024]{1,0:T(8,128)(2,1)} %get-tuple-element.12.a_in, bf16[192,1024]{1,0:T(8,128)(2,1)} %get-tuple-element.13.b_in, bf16[192,1024]{1,0:T(8,128)(2,1)} %get-tuple-element.14.c_in, ...), custom_call_target="tpu_custom_call" | custom-call | tf_op jit(solution)/shard_map/pallas_call | solution.py:420

commit v3 on v2

--- a/solution.py
+++ b/solution.py
@@ -9,8 +9,9 @@
 
 HD = 64
 RAD = 6
-LANES = 128
-AHEAD = 3
+LANES = 256
+AHEAD = 2
+TILE = 256
 MASKED = -1e30
 MESH = pl.DeviceIdType.MESH
 
@@ -83,7 +84,7 @@
 
 def kernel(
     dims, q_hbm, k_hbm, v_hbm, g_hbm, att_hbm, dq_hbm, dk_hbm, dv_hbm,
-    att_ref, dq_ref, dk_ref, dv_ref, q_ref, k_ref, v_ref, g_ref, edge_ref, edge_t_ref, corner_ref, corner_t_ref, bias, keys, got_lat, put_edge, got_edge, put_corner, got_corner, put_side, got_side, put_lat, got_back,
+    att_ref, dq_ref, dk_ref, dv_ref, q_ref, k_ref, v_ref, g_ref, edge_ref, edge_t_ref, corner_ref, corner_t_ref, bias, chances, bends, keys, got_lat, put_edge, got_edge, put_corner, got_corner, put_side, got_side, put_lat, got_back,
     own, lat_sum, load_sem, save_sem, lat_s, lat_r, edge_s, edge_r, corner_s, corner_r, side_s, side_r, back_s, back_r,
 ):
     rows, cols, slots, n_lat, n_lon, n_head, chunks = dims
@@ -282,15 +283,19 @@
         query_block = by_head(q_ref[:, lanes])
         grad_block = by_head(g_ref[:, lanes])
         scale = HD ** -0.5
-        scores = dot(key_block, query_block, 1, 1) * scale + bias[...]
-        weights = jnp.exp(scores - jnp.max(scores, axis=0, keepdims=True))
-        weights = weights * (1.0 / jnp.sum(weights, axis=0, keepdims=True))
-        probabilities = weights.astype(jnp.bfloat16)
+        for first in range(0, heads * tokens, TILE):
+            at = pl.ds(first, TILE)
+            scores = dot(key_block, query_block[first : first + TILE], 1, 1) * scale + bias[:, at]
+            weights = jnp.exp(scores - jnp.max(scores, axis=0, keepdims=True))
+            weights = weights * (1.0 / jnp.sum(weights, axis=0, keepdims=True))
+            rounded = weights.astype(jnp.bfloat16)
+            chances[:, at] = rounded
+            along = dot(value_block, grad_block[first : first + TILE], 1, 1)
+            weights = rounded.astype(jnp.float32)
+            row_dot = jnp.sum(weights * along, axis=0, keepdims=True)
+            bends[:, at] = (weights * (along - row_dot)).astype(jnp.bfloat16)
+        probabilities, slopes = chances[...], bends[...]
         value_term = dot(probabilities, grad_block)
-        along = dot(value_block, grad_block, 1, 1)
-        weights = probabilities.astype(jnp.float32)
-        row_dot = jnp.sum(weights * along, axis=0, keepdims=True)
-        slopes = (weights * (along - row_dot)).astype(jnp.bfloat16)
         key_term = dot(slopes, query_block) * scale
         for half, term in enumerate((key_term, value_term)):
             at = pl.ds(half * LANES, LANES)
@@ -340,11 +345,11 @@
             copy.start()
 
     def step(t, carry):
-        for delay, stage in ((0, spread_corners), (1, attend), (3, gather_sides), (5, finish)):
+        for delay, stage in ((0, spread_corners), (1, attend), (2, gather_sides), (3, finish)):
             pl.when((t >= delay) & (t < chunks + delay))(functools.partial(stage, t - delay))
         return carry
 
-    lax.fori_loop(0, chunks + 5, step, 0)
+    lax.fori_loop(0, chunks + 3, step, 0)
 
     def drain(g, carry):
         for copy in lat_copies(g) + edge_copies(g) + corner_copies(g) + side_copies(g) + back_copies(g):
@@ -396,6 +401,8 @@
             pltpu.VMEM((2 * corner, strip), bf16),
             pltpu.VMEM((strip, 2 * corner), bf16),
             pltpu.VMEM((count, LANES // HD * tokens), f32),
+            pltpu.VMEM((count, LANES // HD * tokens), bf16),
+            pltpu.VMEM((count, LANES // HD * tokens), bf16),
             pltpu.VMEM((count, wide), bf16),
             pltpu.VMEM((chunks, slots, strip, wide), bf16),
             pltpu.VMEM((chunks, 2, edge, wide), bf16),

time: 51.4 us -> 49.9 us (0.971)
  Pallas kernels: 50.6 us -> 48.8 us
    pallas_call x1, Pallas kernels: 48.4 us -> 46.6 us  [local(): pl.pallas_call(functools.partial(kernel, (rows, cols, slots, n_lat, n_lon...]
where the time goes in v3:
time: 49.9 us; the launch traced here: 49.4 us
  Pallas kernels  48.8 us (98%)
  between operations  0.64 us (1%)
    pallas_call x1, Pallas kernels, local(): pl.pallas_call(functools.partial(kernel, (rows, cols, slots, n_lat, n_lon...  46.6 us
    pallas_call x1, Pallas kernels, local(): pl.pallas_call(store, out_shape=[jax.ShapeDtypeStruct((tokens, features),...  2.2 us

profile of v3, /device:TPU:0, one launch (start us, length us, event | category | flops | bytes accessed | tf_op | source)
XLA Modules:
  0.0 49.4 jit_solution(2732749178963402454)
XLA Ops:
  0.6 46.6 %shard_map.75 = (bf16[192,1024]{1,0:T(8,128)(2,1)}, bf16[192,1024]{1,0:T(8,128)(2,1)}, bf16[192,1024]{1,0:T(8,128)(2,1)}, bf16[192,1024]{1,0:T(8,128)(2,1)}) custom-call(bf16[192,1024]{1,0:T(8,128)(2,1)} %bitcast.8, bf16[192,1024]{1,0:T(8,128)(2,1)} %bitcast.9, bf16[192,1024]{1,0:T(8,128)(2,1)} %bitcast.10, bf16[192,1024]{1,0:T(8,128)(2,1)} %bitcast.11), custom_call_target="tpu_custom_call" | custom-call | flops 4831838208 | bytes 3145728 | tf_op jit(solution)/shard_map/pallas_call | solution.py:392
  47.2 2.2 %shard_map.76 = (bf16[192,1024]{1,0:T(8,128)(2,1)}, bf16[192,1024]{1,0:T(8,128)(2,1)}, bf16[192,1024]{1,0:T(8,128)(2,1)}, bf16[192,1024]{1,0:T(8,128)(2,1)}) custom-call(bf16[192,1024]{1,0:T(8,128)(2,1)} %get-tuple-element.12.a_in, bf16[192,1024]{1,0:T(8,128)(2,1)} %get-tuple-element.13.b_in, bf16[192,1024]{1,0:T(8,128)(2,1)} %get-tuple-element.14.c_in, ...), custom_call_target="tpu_custom_call" | custom-call | tf_op jit(solution)/shard_map/pallas_call | solution.py:427

commit v4 on v3

--- a/solution.py
+++ b/solution.py
@@ -205,7 +205,7 @@
         return carry
 
     ahead = min(AHEAD, chunks)
-    lax.fori_loop(0, ahead, start_lat, 0)
+    start_lat(0, 0)
 
     def one_hot(token, place):
         return jnp.where(token == place, 1.0, 0.0).astype(jnp.bfloat16)
@@ -214,8 +214,7 @@
     edge_ref[...] = one_hot(edge_token(counted((n, 1), 0), edge, cols), counted((n, tokens), 1))
     loads[0].wait()
     loads[1].wait()
-    for g in range(ahead):
-        send_edges(g)
+    send_edges(0)
     edge_t_ref[...] = one_hot(edge_token(counted((1, n), 1), edge, cols), counted((tokens, n), 0))
     n = 2 * corner
     corner_ref[...] = one_hot(corner_token(counted((n, 1), 0), corner, cols), counted((n, strip), 1))
@@ -233,6 +232,9 @@
     if count > used:
         keys[pl.ds(used, count - used), :] = jnp.zeros((count - used, 2 * LANES), jnp.bfloat16)
 
+    for g in range(1, ahead):
+        start_lat(g, 0)
+        send_edges(g)
     loads[2].wait()
     loads[3].wait()
     lane_head = lax.broadcasted_iota(jnp.int32, (tokens, LANES), 1) // HD

time: 49.9 us -> 49.7 us (level)
  no operation moved by 1% of the time
where the time goes in v4:
time: 49.7 us; the launch traced here: 49.4 us
  Pallas kernels  48.8 us (98%)
  between operations  0.64 us (1%)
    pallas_call x1, Pallas kernels, local(): pl.pallas_call(functools.partial(kernel, (rows, cols, slots, n_lat, n_lon...  46.6 us
    pallas_call x1, Pallas kernels, local(): pl.pallas_call(store, out_shape=[jax.ShapeDtypeStruct((tokens, features),...  2.2 us

profile of v4, /device:TPU:0, one launch (start us, length us, event | category | flops | bytes accessed | tf_op | source)
XLA Modules:
  0.0 49.4 jit_solution(11248105755674059783)
XLA Ops:
  0.6 46.6 %shard_map.75 = (bf16[192,1024]{1,0:T(8,128)(2,1)}, bf16[192,1024]{1,0:T(8,128)(2,1)}, bf16[192,1024]{1,0:T(8,128)(2,1)}, bf16[192,1024]{1,0:T(8,128)(2,1)}) custom-call(bf16[192,1024]{1,0:T(8,128)(2,1)} %bitcast.8, bf16[192,1024]{1,0:T(8,128)(2,1)} %bitcast.9, bf16[192,1024]{1,0:T(8,128)(2,1)} %bitcast.10, bf16[192,1024]{1,0:T(8,128)(2,1)} %bitcast.11), custom_call_target="tpu_custom_call" | custom-call | flops 4831838208 | bytes 3145728 | tf_op jit(solution)/shard_map/pallas_call | solution.py:394
  47.2 2.2 %shard_map.76 = (bf16[192,1024]{1,0:T(8,128)(2,1)}, bf16[192,1024]{1,0:T(8,128)(2,1)}, bf16[192,1024]{1,0:T(8,128)(2,1)}, bf16[192,1024]{1,0:T(8,128)(2,1)}) custom-call(bf16[192,1024]{1,0:T(8,128)(2,1)} %get-tuple-element.12.a_in, bf16[192,1024]{1,0:T(8,128)(2,1)} %get-tuple-element.13.b_in, bf16[192,1024]{1,0:T(8,128)(2,1)} %get-tuple-element.14.c_in, ...), custom_call_target="tpu_custom_call" | custom-call | tf_op jit(solution)/shard_map/pallas_call | solution.py:429
